TPU v7x, 256 devices: a whole 4x4x8 slice. The times are simulated.
256 devices in a mesh: block: 16 (over x, z_hi, core), day: 16 (over y, z_lo).
Axes of the slice: x: 4, y: 4, z: 8 (z_hi: 2, z_lo: 4; z = z_hi * 4 + z_lo), core: 2. Of those that a mesh axis runs over, the one named last changes fastest.
Arguments:
- spectra: bfloat16 [16, 8, 256, 2, 4096], P('day', None, 'block'), may hold values from -6 to 6
- hour_mask: int32 [16, 8, 256], P('day', None, 'block'), may hold values 0 or 1
- pairs: int32 [16, 2], replicated, may hold values from 0 to 15, as said below
Outputs:
- correlation: float32 [16, 256, 2048], P('block', 'day')
Inputs may be any that keep to these rules, and one draw needn't show every extreme that they name: `pairs`: rows k * 8 to (k + 1) * 8 - 1 form round k: every block appears in exactly one of its rows, so the two entries of a row differ.
All inputs are finite; a program needn't handle non-finite values. No bound on the sum of `hour_mask` on one device may be relied on, other than what follows from the above.
Results may differ from a plain program's by a relative error of at most 0.004.
Values may be sent and summed in bfloat16 or wider, within the bound.
No kernel may reach another device: no remote copies, remote signals or barrier semaphores. Data moves between devices by JAX's collectives and lax.ppermute only.
A program may use at most 128 MiB of HBM per device.

v0:
```python
import math
import jax
import jax.numpy as jnp
from jax import lax
from jax.sharding import PartitionSpec as P

F = 4096
LAGS = 2048


def tables(first, count, lags, width):
    bins = first + jnp.arange(count, dtype=jnp.int32)
    shifts = jnp.arange(lags, dtype=jnp.int32) - lags // 2
    turns = jnp.mod((bins + 1)[:, None] * shifts[None, :], 2 * width)
    phase = turns.astype(jnp.float32) * (math.pi / width)
    return (jnp.cos(phase), jnp.sin(phase))


def cross_terms(left, right):
    left_re = left[:, :, :, None, 0].astype(jnp.float32)
    left_im = left[:, :, :, None, 1].astype(jnp.float32)
    right_re = right[:, :, None, :, 0].astype(jnp.float32)
    right_im = right[:, :, None, :, 1].astype(jnp.float32)
    cross_re = jnp.sum(left_re * right_re + left_im * right_im, axis=0)
    cross_im = jnp.sum(left_im * right_re - left_re * right_im, axis=0)
    return (cross_re, cross_im)


def shards(spectra, hour_mask, pairs):
    blocks_count = lax.axis_size("block")
    days_count = lax.axis_size("day") * spectra.shape[0]
    stations = spectra.shape[2]
    values = spectra[0].astype(jnp.float32)
    power = jnp.mean(values[:, :, 0] * values[:, :, 0] + values[:, :, 1] * values[:, :, 1], axis=-1)
    factor = hour_mask[0].astype(jnp.float32) / jnp.sqrt(power + 1e-06)
    whitened = (values * factor[:, :, None, None]).astype(jnp.bfloat16)
    spread = lax.all_to_all(whitened, "block", split_axis=3, concat_axis=1, tiled=True)
    hours = spread.shape[0]
    band_part = spread.shape[3]
    grouped = spread.reshape(hours, blocks_count, stations, 2, band_part)
    left = jnp.take(grouped, pairs[:, 0], axis=1)
    right = jnp.take(grouped, pairs[:, 1], axis=1)
    cross_re, cross_im = cross_terms(left, right)
    pair_count = cross_re.shape[0]
    cross_re = cross_re.reshape(pair_count, stations * stations, band_part)
    cross_im = cross_im.reshape(pair_count, stations * stations, band_part)
    scale = 1.0 / math.sqrt(F * hours * days_count)
    high = lax.Precision.HIGHEST
    summed_re, summed_im = (
        lax.psum_scatter(cross_re, "day", scatter_dimension=1, tiled=True),
        lax.psum_scatter(cross_im, "day", scatter_dimension=1, tiled=True),
    )
    row_count = summed_re.shape[1]
    offset = lax.axis_index("block") * band_part
    cos_table, sin_table = tables(offset, band_part, LAGS, F)
    flat_re = summed_re.reshape(-1, band_part)
    flat_im = summed_im.reshape(-1, band_part)
    lagged = jnp.dot(flat_re, cos_table, precision=high) - jnp.dot(
        flat_im, sin_table, precision=high
    )
    result = lax.psum_scatter(lagged * scale, "block", scatter_dimension=0, tiled=True)
    return result.reshape(pair_count // blocks_count, row_count, LAGS)


def solution(mesh):
    in_specs = (P("day", None, "block", None, None), P("day", None, "block"), P())
    out_specs = P("block", "day", None)
    return jax.shard_map(shards, mesh=mesh, in_specs=in_specs, out_specs=out_specs, check_vma=False)
```

profile of v0, /device:TPU:8, one launch (start us, length us, event | category | flops | bytes accessed | tf_op | source)
XLA Modules:
  0.0 524.4 jit_solution(7528432776630027660)
XLA Ops:
  6.5 21.7 %copy.32 = bf16[1,8,16,2,4096]{2,1,3,4,0:T(8,128)(2,1)} copy(bf16[1,8,16,2,4096]{4,3,2,1,0:T(2,128)(2,1)} %param.5) | data formatting | bytes 4194304 | tf_op args[0]
  28.2 0.0 slice-start
  28.2 0.0 slice-start.1
  28.2 0.0 slice-start.2
  28.2 21.6 %bitcast_convert_fusion = f32[8,16,2,4096]{1,0,2,3:T(8,128)} fusion(bf16[1,8,16,2,4096]{2,1,3,4,0:T(8,128)(2,1)} %copy.32), kind=kLoop, calls=%fused_computation.9 | loop fusion | flops 1048576 | bytes 6291456 | tf_op jit(solution)/shard_map/convert_element_type | solution.py:33
  49.8 0.0 copy-start
  49.8 0.0 slice-start.3
  49.8 12.1 %fusion.1 = f32[8,16]{1,0:T(8,128)S(1)} fusion(f32[8,16,2,4096]{1,0,2,3:T(8,128)} %bitcast_convert_fusion), kind=kLoop, calls=%fused_computation.7 | loop fusion | flops 2097024 | bytes 4194816 | tf_op jit(solution)/shard_map/reduce_sum | solution.py:34
  61.9 0.0 copy-done
  61.9 0.0 slice-done
  61.9 0.0 slice-done.1
  61.9 0.0 slice-done.2
  61.9 0.0 slice-done.3
  62.0 7.6 %fusion.23 = bf16[4096,2,8,16]{3,2,1,0:T(8,128)(2,1)} fusion(f32[8,16]{1,0:T(8,128)S(1)} %bitcast_multiply_fusion, bf16[1,8,16,2,4096]{2,1,3,4,0:T(8,128)(2,1)S(1)} %bitcast.52), kind=kLoop, calls=%fused_computation.50 | loop fusion | flops 3145728 | bytes 4194816
  69.6 20.8 %reshape.98 = bf16[16,2,32768]{2,1,0:T(2,128)(2,1)} reshape(bf16[4096,2,8,16]{3,2,1,0:T(8,128)(2,1)} %fusion.23) | data formatting | bytes 4194304
  90.4 0.0 copy-start.1
  90.4 11.2 %all-to-all-start = ((bf16[16,2,32768]{2,1,0:T(2,128)(2,1)}), bf16[16,2,32768]{2,1,0:T(2,128)(2,1)S(1)}, u32[]{:S(2)}, u32[]{:S(2)}) async-start(bf16[16,2,32768]{2,1,0:T(2,128)(2,1)} %reshape.98), calls=%async_computation | async-start | bytes 4194304 | tf_op jit(solution)/shard_map/all_to_all | solution.py:37
  101.5 0.0 reduce-scatter.4.cloned.1.call-start
  101.6 0.0 copy-done.1
  101.6 53.3 %all-to-all-done = bf16[16,2,32768]{2,1,0:T(2,128)(2,1)S(1)} async-done(((bf16[16,2,32768]{2,1,0:T(2,128)(2,1)}), bf16[16,2,32768]{2,1,0:T(2,128)(2,1)S(1)}, u32[]{:S(2)}, u32[]{:S(2)}) %all-to-all-start) | async-done | bytes 2097184 | tf_op jit(solution)/shard_map/all_to_all | solution.py:37
  155.0 14.3 %reshape.99 = bf16[4096,2,8,16]{3,2,1,0:T(8,128)(2,1)} reshape(bf16[16,2,32768]{2,1,0:T(2,128)(2,1)S(1)} %all-to-all-done) | data formatting | bytes 4194304
  169.2 17.1 %copy.34 = bf16[8,16,2,16,256]{4,1,2,3,0:T(8,128)(2,1)S(1)} copy(bf16[8,16,2,16,256]{1,0,2,4,3:T(8,128)(2,1)} %bitcast.53) | data formatting | bytes 4194304 | tf_op jit(solution)/shard_map/all_to_all | solution.py:37
  186.3 2.0 gather_fusion
  188.3 2.0 gather_fusion.1
  190.3 2.6 select_bitcast_fusion
  193.0 0.6 fusion.12
  193.6 1.7 fusion.11
  195.4 23.3 %subtract_reduce_fusion = (f32[16,16,16,256]{3,2,1,0:T(8,128)}, f32[16,16,16,256]{3,2,1,0:T(8,128)}) fusion(f32[8,16,16,256]{3,2,0,1:T(8,128)S(1)} %get-tuple-element.12, f32[8,16,16,256]{3,2,0,1:T(8,128)S(1)} %get-tuple-element.14, f32[8,16,16,256]{3,2,0,1:T(8,128)S(1)} %get-tuple-element.13, f32[8,16,16,256]{3,2,0,1:T(8,128)} %get-tuple-element.15), kind=kLoop, calls=%fused_computation.2 | loop fusion | flops 65011712 | bytes 16777216 | tf_op jit(solution)/shard_map/reduce_sum | solution.py:25
  218.7 0.0 reduce-scatter.4.cloned.1.call-update
  218.7 0.0 reduce-scatter.6.cloned.1.call-start
  218.8 0.7 reduce-scatter.6.cloned.1.call-update
  219.5 0.2 reduce-scatter.8.cloned.1.call-start
  219.7 95.2 %reduce-scatter.4.cloned.1.call-done = f32[16,16,256]{2,1,0:T(8,128)} async-done(((f32[16,256,256]{2,1,0:T(8,128)}), f32[16,16,256]{2,1,0:T(8,128)}) %reduce-scatter.4.cloned.1.call-update) | async-done | bytes 262160 | tf_op jit(solution)/shard_map/reduce_scatter | solution.py:50
  314.9 10.4 %fusion.7 = f32[256,2048]{1,0:T(8,128)S(1)} fusion(f32[256,256]{1,0:T(8,128)} %bitcast.58, s32[2048]{0:T(1024)S(1)} %iota_add_fusion, s32[256]{0:T(256)S(1)} %add_add_fusion), kind=kOutput, calls=%fused_computation.23 | convolution fusion | flops 1617952768 | bytes 2368512 | tf_op jit(solution)/shard_map/dot_general | solution.py:58
  325.3 92.5 %reduce-scatter.6.cloned.1.call-done = f32[16,16,256]{2,1,0:T(8,128)} async-done(((f32[16,256,256]{2,1,0:T(8,128)}), f32[16,16,256]{2,1,0:T(8,128)}) %reduce-scatter.6.cloned.1.call-update) | async-done | bytes 262160 | tf_op jit(solution)/shard_map/reduce_scatter | solution.py:51
  417.8 11.9 %fusion.2 = f32[256,2048]{1,0:T(8,128)} fusion(f32[256,2048]{1,0:T(8,128)S(1)} %fusion.7, f32[256,256]{1,0:T(8,128)} %bitcast.59, s32[2048]{0:T(1024)S(1)} %iota_add_fusion, s32[256]{0:T(256)S(1)} %add_add_fusion), kind=kOutput, calls=%fused_computation.16 | convolution fusion | flops 1619001344 | bytes 4465664 | tf_op jit(solution)/shard_map/dot_general | solution.py:58
  429.7 0.0 reduce-scatter.8.cloned.1.call-update
  429.8 88.1 %reduce-scatter.8.cloned.1.call-done = f32[16,2048]{1,0:T(8,128)} async-done(((f32[256,2048]{1,0:T(8,128)}), f32[16,2048]{1,0:T(8,128)}) %reduce-scatter.8.cloned.1.call-update) | async-done | bytes 131088 | tf_op jit(solution)/shard_map/reduce_scatter | solution.py:61
  (7 shorter events, 0.0 us)
Async XLA Ops:
  28.2 33.7 %slice-start = ((s8[16777216]{0:T(1024)(128)(4,1)}), s8[4194304]{0:T(1024)(128)(4,1)S(1)}, s32[]{:S(2)}) async-start(s8[16777216]{0:T(1024)(128)(4,1)} %bitcast.51), calls=%async_computation.7 | async-start | bytes 8388608
  28.2 33.7 %slice-start.1 = ((s8[16777216]{0:T(1024)(128)(4,1)}), s8[4194304]{0:T(1024)(128)(4,1)S(1)}, s32[]{:S(2)}) async-start(s8[16777216]{0:T(1024)(128)(4,1)} %bitcast.51), calls=%async_computation.8 | async-start | bytes 8388608
  28.2 33.7 %slice-start.2 = ((s8[16777216]{0:T(1024)(128)(4,1)}), s8[4194304]{0:T(1024)(128)(4,1)S(1)}, s32[]{:S(2)}) async-start(s8[16777216]{0:T(1024)(128)(4,1)} %bitcast.51), calls=%async_computation.9 | async-start | bytes 8388608
  49.8 12.1 %copy-start = (s32[1,8,16]{2,1,0:T(8,128)S(1)}, s32[1,8,16]{2,1,0:T(8,128)}, u32[]{:S(2)}) copy-start(s32[1,8,16]{2,1,0:T(8,128)} %param.6) | copy-start | bytes 1540
  49.8 12.1 %slice-start.3 = ((s8[16777216]{0:T(1024)(128)(4,1)}), s8[4194304]{0:T(1024)(128)(4,1)S(1)}, s32[]{:S(2)}) async-start(s8[16777216]{0:T(1024)(128)(4,1)} %bitcast.51), calls=%async_computation.10 | async-start | bytes 8388608
  90.4 11.2 %copy-start.1 = (s32[16,2]{0,1:T(2,128)S(1)}, s32[16,2]{0,1:T(2,128)}, u32[]{:S(2)}) copy-start(s32[16,2]{0,1:T(2,128)} %param.7) | copy-start | bytes 388
  90.4 64.6 %all-to-all-start = ((bf16[16,2,32768]{2,1,0:T(2,128)(2,1)}), bf16[16,2,32768]{2,1,0:T(2,128)(2,1)S(1)}, u32[]{:S(2)}, u32[]{:S(2)}) async-start(bf16[16,2,32768]{2,1,0:T(2,128)(2,1)} %reshape.98), calls=%async_computation | async-start | bytes 4194304 | tf_op jit(solution)/shard_map/all_to_all | solution.py:37
  101.5 213.3 %reduce-scatter.4.cloned.1.call-start = ((), (), s32[]{:S(2)}) async-start(), calls=%async_computation.4 | async-start | bytes 4456448 | tf_op jit(solution)/shard_map/reduce_scatter | solution.py:50
  218.7 199.1 %reduce-scatter.6.cloned.1.call-start = ((), (), s32[]{:S(2)}) async-start(), calls=%async_computation.5 | async-start | bytes 4456448 | tf_op jit(solution)/shard_map/reduce_scatter | solution.py:51
  219.5 298.4 %reduce-scatter.8.cloned.1.call-start = ((), (), s32[]{:S(2)}) async-start(), calls=%async_computation.6 | async-start | bytes 2228224 | tf_op jit(solution)/shard_map/reduce_scatter | solution.py:61
Sparse Core Ops, SparseCore 0:
  218.8 95.9 reduce-scatter.3
  317.4 100.3 reduce-scatter.5
  429.9 87.8 reduce-scatter.7
where the time goes:
time: 525 us; the launch traced here: 524 us
  waiting for transfers between devices  330 us (63%)
  local copies, waits for them, and re-layouts  77.8 us (15%)
  other arithmetic  69.7 us (13%)
  matrix products  22.4 us (4%)
  between operations  13.3 us (3%)
  starting transfers between devices  11.5 us (2%)
    reduce_scatter x1, waiting for transfers between devices, shards(): lax.psum_scatter(cross_re, 'day', scatter_dimension=1, tiled=True)  95.2 us
    reduce_scatter x1, waiting for transfers between devices, shards(): lax.psum_scatter(cross_im, 'day', scatter_dimension=1, tiled=True)  92.5 us
    reduce_scatter x1, waiting for transfers between devices, shards(): lax.psum_scatter(lagged * scale, 'block', scatter_dimension=0, tiled=True)  88.1 us
    unnamed x15, local copies, waits for them, and re-layouts  56.7 us
    all_to_all x1, waiting for transfers between devices, shards(): lax.all_to_all(whitened, 'block', split_axis=3, concat_axis=1, tiled=True)  53.3 us
    reduce_sum x1, other arithmetic, cross_terms(): cross_im = jnp.sum(left_im * right_re - left_re * right_im, axis=0)  23.3 us
    convert_element_type x1, other arithmetic, shards(): values = spectra[0].astype(jnp.float32)  21.6 us
    all_to_all x1, local copies, waits for them, and re-layouts, shards(): lax.all_to_all(whitened, 'block', split_axis=3, concat_axis=1, tiled=True)  17.1 us
  transfers between devices with their start and end apart: 4, of which 4 were waited for; matrix products, arithmetic and copies ran while one was open for 2% of the time, Pallas kernels for 0%

commit v1 on v0

--- a/solution.py
+++ b/solution.py
@@ -34,7 +34,9 @@
     power = jnp.mean(values[:, :, 0] * values[:, :, 0] + values[:, :, 1] * values[:, :, 1], axis=-1)
     factor = hour_mask[0].astype(jnp.float32) / jnp.sqrt(power + 1e-06)
     whitened = (values * factor[:, :, None, None]).astype(jnp.bfloat16)
-    spread = lax.all_to_all(whitened, "block", split_axis=3, concat_axis=1, tiled=True)
+    pieces = jnp.split(whitened, lax.axis_size("block"), axis=3)
+    received = lax.all_to_all(jnp.stack(pieces), "block", 0, 0)
+    spread = jnp.concatenate(received, axis=1)
     hours = spread.shape[0]
     band_part = spread.shape[3]
     grouped = spread.reshape(hours, blocks_count, stations, 2, band_part)

time: 525 us -> 457 us (0.87); the launches traced: 524 us -> 450 us
  local copies, waits for them, and re-layouts: 77.8 us -> 29.1 us
  other arithmetic: 69.7 us -> 44 us
    unnamed x15 -> x21, local copies, waits for them, and re-layouts: 56.7 us -> 11.7 us
    convert_element_type x1, other arithmetic: 21.6 us -> 3.56 us  [shards(): values = spectra[0].astype(jnp.float32)]
    all_to_all x1 -> x0, local copies, waits for them, and re-layouts: 17.1 us -> none  [shards(): lax.all_to_all(whitened, 'block', split_axis=3, concat_axis=1, tiled=True)]
    unnamed x2 -> x0, other arithmetic: 7.61 us -> none
    reduce_sum x1, other arithmetic: 12.1 us -> 4.78 us  [shards(): jnp.mean(values[:, :, 0] * values[:, :, 0] + values[:, :, 1] * values[:,...]
    reduce_sum x1, other arithmetic: 23.3 us -> 16.2 us  [cross_terms(): cross_im = jnp.sum(left_im * right_re - left_re * right_im, axis=0)]
where the time goes in v1:
time: 457 us; the launch traced here: 450 us
  waiting for transfers between devices  329 us (72%)
  other arithmetic  44 us (10%)
  local copies, waits for them, and re-layouts  29.1 us (6%)
  matrix products  22.5 us (5%)
  between operations  13.5 us (3%)
  starting transfers between devices  11.7 us (3%)
    reduce_scatter x1, waiting for transfers between devices, shards(): lax.psum_scatter(cross_re, 'day', scatter_dimension=1, tiled=True)  95.3 us
    reduce_scatter x1, waiting for transfers between devices, shards(): lax.psum_scatter(cross_im, 'day', scatter_dimension=1, tiled=True)  92.5 us
    reduce_scatter x1, waiting for transfers between devices, shards(): lax.psum_scatter(lagged * scale, 'block', scatter_dimension=0, tiled=True)  88.1 us
    all_to_all x1, waiting for transfers between devices, shards(): received = lax.all_to_all(jnp.stack(pieces), 'block', 0, 0)  52.9 us
    reduce_sum x1, other arithmetic, cross_terms(): cross_im = jnp.sum(left_im * right_re - left_re * right_im, axis=0)  16.2 us
    dot_general x1, matrix products, shards(): jnp.dot(flat_im, sin_table, precision=high)  12.1 us
    unnamed x21, local copies, waits for them, and re-layouts  11.7 us
    all_to_all x1, starting transfers between devices, shards(): received = lax.all_to_all(jnp.stack(pieces), 'block', 0, 0)  11.2 us
  transfers between devices with their start and end apart: 4, of which 4 were waited for; matrix products, arithmetic and copies ran while one was open for 2% of the time, Pallas kernels for 0%

profile of v1, /device:TPU:8, one launch (start us, length us, event | category | flops | bytes accessed | tf_op | source)
XLA Modules:
  0.0 450.3 jit_solution(5404549512218910900)
XLA Ops:
  6.5 3.6 bitcast_convert_fusion
  10.1 0.0 copy-start.1
  10.1 0.0 copy-start
  10.1 4.8 %fusion.10 = f32[8,16]{1,0:T(8,128)S(1)} fusion(f32[8,16,2,4096]{3,2,1,0:T(2,128)S(1)} %bitcast_convert_fusion), kind=kLoop, calls=%fused_computation.34 | loop fusion | flops 2097024 | bytes 4194816 | tf_op jit(solution)/shard_map/reduce_sum | solution.py:34
  14.9 0.0 copy-done.1
  14.9 0.0 copy-done
  14.9 3.9 multiply_convert_fusion
  18.8 0.8 fusion.28
  19.6 0.8 fusion.27
  20.3 0.8 fusion.26
  21.1 0.8 fusion.25
  21.9 0.8 fusion.24
  22.7 0.8 fusion.23
  23.4 0.8 fusion.22
  24.2 0.8 fusion.21
  25.0 0.8 fusion.20
  25.8 0.8 fusion.19
  26.6 0.8 fusion.18
  27.4 0.8 fusion.17
  28.1 0.8 fusion.16
  28.9 0.8 fusion.15
  29.7 0.8 fusion.14
  30.5 0.8 fusion.13
  31.2 0.0 copy-start.2
  31.2 11.2 %all-to-all-start = ((bf16[16,8,16,2,256]{4,3,2,1,0:T(2,128)(2,1)}), bf16[16,8,16,2,256]{4,3,2,1,0:T(2,128)(2,1)S(1)}, u32[]{:S(2)}, u32[]{:S(2)}) async-start(bf16[16,8,16,2,256]{4,3,2,1,0:T(2,128)(2,1)} %fusion.13), calls=%async_computation | async-start | bytes 4194304 | tf_op jit(solution)/shard_map/all_to_all | solution.py:38
  42.4 0.5 reduce-scatter.4.cloned.1.call-start
  42.9 0.0 copy-done.2
  43.0 52.9 %all-to-all-done = bf16[16,8,16,2,256]{4,3,2,1,0:T(2,128)(2,1)S(1)} async-done(((bf16[16,8,16,2,256]{4,3,2,1,0:T(2,128)(2,1)}), bf16[16,8,16,2,256]{4,3,2,1,0:T(2,128)(2,1)S(1)}, u32[]{:S(2)}, u32[]{:S(2)}) %all-to-all-start) | async-done | bytes 2097184 | tf_op jit(solution)/shard_map/all_to_all | solution.py:38
  95.8 5.9 %gather_fusion = bf16[16,8,16,2,256]{4,3,2,1,0:T(2,128)(2,1)} fusion(bf16[8,16,16,2,256]{4,3,2,0,1:T(2,128)(2,1)S(1)} %bitcast.101, s32[1024]{0:T(1024)S(1)} %pad_clamp_fusion.1), kind=kCustom, calls=%fused_computation.clone | custom fusion | bytes 4194368 | tf_op jit(solution)/shard_map/jit(_take)/gather | solution.py:43
  101.7 5.9 %gather_fusion.1 = bf16[16,8,16,2,256]{4,3,2,1,0:T(2,128)(2,1)} fusion(bf16[8,16,16,2,256]{4,3,2,0,1:T(2,128)(2,1)S(1)} %bitcast.102, s32[1024]{0:T(1024)S(1)} %pad_clamp_fusion), kind=kCustom, calls=%fused_computation.1.clone | custom fusion | bytes 4194368 | tf_op jit(solution)/shard_map/jit(_take)/gather | solution.py:44
  107.6 5.9 %fusion.8 = (bf16[8,16,16,2,256]{4,3,2,0,1:T(2,128)(2,1)S(1)}, bf16[8,16,16,2,256]{4,3,2,0,1:T(2,128)(2,1)S(1)}) fusion(bf16[16,8,16,2,256]{4,3,2,1,0:T(2,128)(2,1)} %gather_fusion, pred[16]{0:T(512)(128)(4,1)S(1)} %get-tuple-element.8, bf16[16,8,16,2,256]{4,3,2,1,0:T(2,128)(2,1)} %gather_fusion.1, pred[16]{0:T(512)(128)(4,1)S(1)} %get-tuple-element.16), kind=kLoop, calls=%fused_computation.32 | loop fusion | flops 2097152 | bytes 8388640 | tf_op jit(solution)/shard_map/jit(_take)/select_n | solution.py:43
  113.5 4.8 %slice_convert_fusion.3 = (f32[8,16,16,1,256]{4,3,2,0,1:T(1,128)S(1)}, f32[8,16,16,1,256]{4,3,2,0,1:T(1,128)S(1)}) fusion(bf16[8,16,16,2,256]{4,3,2,0,1:T(2,128)(2,1)S(1)} %get-tuple-element.18), kind=kLoop, calls=%fused_computation.20 | loop fusion | flops 1048576 | bytes 6291456 | tf_op jit(solution)/shard_map/mul | solution.py:24
  118.3 0.2 copy.23
  118.6 4.8 %slice_convert_fusion.2 = (f32[8,16,16,1,256]{4,3,2,0,1:T(1,128)S(1)}, f32[8,16,16,1,256]{4,3,2,0,1:T(1,128)S(1)}) fusion(bf16[8,16,16,2,256]{4,3,2,0,1:T(2,128)(2,1)S(1)} %get-tuple-element.19), kind=kLoop, calls=%fused_computation.19 | loop fusion | flops 1048576 | bytes 6291456 | tf_op jit(solution)/shard_map/convert_element_type | solution.py:22
  123.3 1.6 copy.20
  125.0 1.5 copy.21
  126.5 1.6 copy.22
  128.0 16.2 %subtract_reduce_fusion = (f32[16,16,16,256]{3,2,1,0:T(8,128)}, f32[16,16,16,256]{3,2,1,0:T(8,128)}) fusion(f32[8,16,16,256]{3,2,1,0:T(8,128)} %bitcast.106, f32[8,16,16,256]{3,2,1,0:T(8,128)} %bitcast.107, f32[8,16,16,256]{3,2,1,0:T(8,128)} %bitcast.108, f32[8,16,16,256]{3,2,1,0:T(8,128)S(1)} %bitcast.105), kind=kLoop, calls=%fused_computation.2 | loop fusion | flops 65011712 | bytes 16777216 | tf_op jit(solution)/shard_map/reduce_sum | solution.py:25
  144.2 0.0 reduce-scatter.4.cloned.1.call-update
  144.3 0.0 reduce-scatter.6.cloned.1.call-start
  144.3 0.7 reduce-scatter.6.cloned.1.call-update
  145.0 0.0 reduce-scatter.8.cloned.1.call-start
  145.1 95.3 %reduce-scatter.4.cloned.1.call-done = f32[16,16,256]{2,1,0:T(8,128)} async-done(((f32[16,256,256]{2,1,0:T(8,128)}), f32[16,16,256]{2,1,0:T(8,128)}) %reduce-scatter.4.cloned.1.call-update) | async-done | bytes 262160 | tf_op jit(solution)/shard_map/reduce_scatter | solution.py:52
  240.4 10.4 %fusion.6 = f32[256,2048]{1,0:T(8,128)S(1)} fusion(f32[256,256]{1,0:T(8,128)} %bitcast.109, s32[2048]{0:T(1024)S(1)} %iota_add_fusion, s32[256]{0:T(256)S(1)} %add_add_fusion), kind=kOutput, calls=%fused_computation.30 | convolution fusion | flops 1617952768 | bytes 2368512 | tf_op jit(solution)/shard_map/dot_general | solution.py:60
  250.9 92.5 %reduce-scatter.6.cloned.1.call-done = f32[16,16,256]{2,1,0:T(8,128)} async-done(((f32[16,256,256]{2,1,0:T(8,128)}), f32[16,16,256]{2,1,0:T(8,128)}) %reduce-scatter.6.cloned.1.call-update) | async-done | bytes 262160 | tf_op jit(solution)/shard_map/reduce_scatter | solution.py:53
  343.4 12.1 %fusion = f32[256,2048]{1,0:T(8,128)} fusion(f32[256,2048]{1,0:T(8,128)S(1)} %fusion.6, f32[256,256]{1,0:T(8,128)} %bitcast.110, s32[2048]{0:T(1024)S(1)} %iota_add_fusion, s32[256]{0:T(256)S(1)} %add_add_fusion), kind=kOutput, calls=%fused_computation.13 | convolution fusion | flops 1619001344 | bytes 4465664 | tf_op jit(solution)/shard_map/dot_general | solution.py:60
  355.4 0.0 reduce-scatter.8.cloned.1.call-update
  355.5 88.1 %reduce-scatter.8.cloned.1.call-done = f32[16,2048]{1,0:T(8,128)} async-done(((f32[256,2048]{1,0:T(8,128)}), f32[16,2048]{1,0:T(8,128)}) %reduce-scatter.8.cloned.1.call-update) | async-done | bytes 131088 | tf_op jit(solution)/shard_map/reduce_scatter | solution.py:63
  (6 shorter events, 0.0 us)
Async XLA Ops:
  10.1 4.8 %copy-start.1 = (s32[1,8,16]{2,1,0:T(8,128)S(1)}, s32[1,8,16]{2,1,0:T(8,128)}, u32[]{:S(2)}) copy-start(s32[1,8,16]{2,1,0:T(8,128)} %param.6) | copy-start | bytes 1540
  10.1 4.8 %copy-start = (bf16[1,8,16,2,4096]{4,3,2,1,0:T(2,128)(2,1)S(1)}, bf16[1,8,16,2,4096]{4,3,2,1,0:T(2,128)(2,1)}, u32[]{:S(2)}) copy-start(bf16[1,8,16,2,4096]{4,3,2,1,0:T(2,128)(2,1)} %param.5) | copy-start | bytes 6291460
  31.2 11.7 %copy-start.2 = (s32[16,2]{0,1:T(2,128)S(1)}, s32[16,2]{0,1:T(2,128)}, u32[]{:S(2)}) copy-start(s32[16,2]{0,1:T(2,128)} %param.7) | copy-start | bytes 388
  31.2 64.6 %all-to-all-start = ((bf16[16,8,16,2,256]{4,3,2,1,0:T(2,128)(2,1)}), bf16[16,8,16,2,256]{4,3,2,1,0:T(2,128)(2,1)S(1)}, u32[]{:S(2)}, u32[]{:S(2)}) async-start(bf16[16,8,16,2,256]{4,3,2,1,0:T(2,128)(2,1)} %fusion.13), calls=%async_computation | async-start | bytes 4194304 | tf_op jit(solution)/shard_map/all_to_all | solution.py:38
  42.4 198.0 %reduce-scatter.4.cloned.1.call-start = ((), (), s32[]{:S(2)}) async-start(), calls=%async_computation.4 | async-start | bytes 4456448 | tf_op jit(solution)/shard_map/reduce_scatter | solution.py:52
  144.3 199.1 %reduce-scatter.6.cloned.1.call-start = ((), (), s32[]{:S(2)}) async-start(), calls=%async_computation.5 | async-start | bytes 4456448 | tf_op jit(solution)/shard_map/reduce_scatter | solution.py:53
  145.0 298.5 %reduce-scatter.8.cloned.1.call-start = ((), (), s32[]{:S(2)}) async-start(), calls=%async_computation.6 | async-start | bytes 2228224 | tf_op jit(solution)/shard_map/reduce_scatter | solution.py:63
Sparse Core Ops, SparseCore 0:
  144.4 95.9 reduce-scatter.3
  243.0 100.3 reduce-scatter.5
  355.6 87.9 reduce-scatter.7
